TPU v7x, 128 devices: a whole 4x4x4 slice. The times are simulated.
128 devices in a mesh: rows: 32 (over x_hi, y, z), text: 4 (over x_lo, core).
Axes of the slice: x: 4 (x_hi: 2, x_lo: 2; x = x_hi * 2 + x_lo), y: 4, z: 4, core: 2. Of those that a mesh axis runs over, the one named last changes fastest.
Arguments:
- image_tokens: bfloat16 [32, 512, 2048], P('rows', 'text'), may hold values from -6 to 6
- caption_embed: bfloat16 [32, 32, 4096], P('rows', 'text'), may hold values from -6 to 6
- caption_lengths: int32 [32, 2], P('rows'), may hold values from 5 to 16, as said below
- output_grad: bfloat16 [32, 512, 2048], P('rows', 'text'), may hold values from -6 to 6
- norm_self: bfloat16 [2048], P('rows'), may hold values from 0.5 to 1.5
- norm_cross: bfloat16 [2048], P('rows'), may hold values from 0.5 to 1.5
- norm_feed: bfloat16 [2048], P('rows'), may hold values from 0.5 to 1.5
- self_query: bfloat16 [2048, 2048], P('rows', 'text'), may hold values from -0.125 to 0.125
- self_key: bfloat16 [2048, 2048], P('rows', 'text'), may hold values from -0.125 to 0.125
- self_value: bfloat16 [2048, 2048], P('rows', 'text'), may hold values from -0.125 to 0.125
- self_output: bfloat16 [2048, 2048], P('text', 'rows'), may hold values from -1.5 to 1.5
- cross_query: bfloat16 [2048, 2048], P('rows', 'text'), may hold values from -0.125 to 0.125
- cross_key: bfloat16 [4096, 2048], P('rows', 'text'), may hold values from -0.09375 to 0.09375
- cross_value: bfloat16 [4096, 2048], P('rows', 'text'), may hold values from -0.09375 to 0.09375
- cross_output: bfloat16 [2048, 2048], P('text', 'rows'), may hold values from -0.375 to 0.375
- up_weight: bfloat16 [2048, 8192], P('rows', 'text'), may hold values from -0.125 to 0.125
- down_weight: bfloat16 [8192, 2048], P('text', 'rows'), may hold values from -0.0625 to 0.0625
Outputs:
- layer_output_array: bfloat16 [32, 512, 2048], P('rows', 'text')
- image_grad: float32 [32, 512, 2048], P('rows', 'text')
- caption_grad: float32 [32, 32, 4096], P('rows', 'text')
- norm_self_grad: float32 [2048], P('rows')
- norm_cross_grad: float32 [2048], P('rows')
- norm_feed_grad: float32 [2048], P('rows')
- self_query_grad: float32 [2048, 2048], P('rows', 'text')
- self_key_grad: float32 [2048, 2048], P('rows', 'text')
- self_value_grad: float32 [2048, 2048], P('rows', 'text')
- self_output_grad: float32 [2048, 2048], P('text', 'rows')
- cross_query_grad: float32 [2048, 2048], P('rows', 'text')
- cross_key_grad: float32 [4096, 2048], P('rows', 'text')
- cross_value_grad: float32 [4096, 2048], P('rows', 'text')
- cross_output_grad: float32 [2048, 2048], P('text', 'rows')
- up_grad: float32 [2048, 8192], P('rows', 'text')
- down_grad: float32 [8192, 2048], P('text', 'rows')
Inputs may be any that keep to these rules, and one draw needn't show every extreme that they name: caption_lengths[r, i] counts the live slots of image i's caption; slots at or past it are padding. Some image has 16 live slots and some has 5.
All inputs are finite; a program needn't handle non-finite values.
Results may differ from a plain program's by a relative error of at most 0.029.
Values may be sent and summed in bfloat16 or wider, within the bound.
No kernel may reach another device: no remote copies, remote signals or barrier semaphores. Data moves between devices by JAX's collectives and lax.ppermute only.
A program may use at most 192 MiB of HBM per device.

v0:
```python
import jax
import jax.numpy as jnp
from jax import lax
from jax.sharding import PartitionSpec as P

HEAD_DIM = 128
IMAGE_TOKENS = 256
PER_ROW = 2
CAP = 16


EPSILON = 1e-05


def layer_stats(resid):
    mean = jnp.mean(resid, -1, keepdims=True)
    centered = resid - mean
    inverse = lax.rsqrt(jnp.mean(centered * centered, -1, keepdims=True) + EPSILON)
    return (centered * inverse, inverse)


def norm_back(grad_norm, normed, inverse, gain):
    scaled = grad_norm * gain
    inner = (
        scaled
        - jnp.mean(scaled, -1, keepdims=True)
        - normed * jnp.mean(scaled * normed, -1, keepdims=True)
    )
    return (inverse * inner, jnp.sum(grad_norm * normed, axis=(0, 1)))


def gelu_back(hidden_pre, grad_act):
    _, pullback = jax.vjp(lambda value_in: jax.nn.gelu(value_in, approximate=False), hidden_pre)
    return pullback(grad_act)[0]


def gather_tokens(normed_low):
    return lax.all_gather(normed_low, "text", axis=1, tiled=True)


def sum_tokens(partial_value):
    return lax.psum_scatter(partial_value, "text", scatter_dimension=1, tiled=True)


def gather_grads(grad_low):
    return lax.all_gather(grad_low, "text", axis=1, tiled=True)


def sum_inputs(partial_value):
    return lax.psum_scatter(
        partial_value.astype(jnp.bfloat16), "text", scatter_dimension=1, tiled=True
    ).astype(jnp.float32)


def product(operand, factor):
    return jnp.einsum("rsd,de->rse", operand, factor, preferred_element_type=jnp.float32)


def project(operand, factor):
    return product(operand, factor).astype(jnp.bfloat16)


def product_back(operand, factor):
    return jnp.einsum("rse,de->rsd", operand, factor, preferred_element_type=jnp.float32)


def contract_product(operand, factor):
    return jnp.einsum("rsd,rse->de", operand, factor, preferred_element_type=jnp.float32)


def split_heads(value_rows, length_limit):
    return value_rows.reshape(
        value_rows.shape[0], PER_ROW, length_limit, value_rows.shape[2] // HEAD_DIM, HEAD_DIM
    )


def join_heads(value_rows):
    shape = value_rows.shape
    return value_rows.reshape(shape[0], shape[1] * shape[2], shape[3] * shape[4])


def scores_of(query_rows, key_rows):
    return jnp.einsum(
        "rbqhe,rbkhe->rbhqk", query_rows, key_rows, preferred_element_type=jnp.float32
    ) * HEAD_DIM ** (-0.5)


def attend_forward(query_rows, key_rows, value_rows, live_slots):
    scores = scores_of(query_rows, key_rows)
    if live_slots is not None:
        scores = jnp.where(live_slots, scores, -1e30)
    row_max = jnp.max(scores, -1, keepdims=True)
    shifted = jnp.exp(scores - row_max)
    row_total = jnp.sum(shifted, -1, keepdims=True)
    attention = (shifted / row_total).astype(jnp.bfloat16)
    mixed = jnp.einsum(
        "rbhqk,rbkhe->rbqhe", attention, value_rows, preferred_element_type=jnp.float32
    )
    return (mixed.astype(jnp.bfloat16), row_max + jnp.log(row_total))


def attend_back(query_rows, key_rows, value_rows, live_slots, logsum, grad_mixed):
    scores = scores_of(query_rows, key_rows)
    attention = jnp.exp(scores - logsum)
    if live_slots is not None:
        attention = jnp.where(live_slots, attention, 0.0)
    grad_values = jnp.einsum(
        "rbhqk,rbqhe->rbkhe",
        attention.astype(jnp.bfloat16),
        grad_mixed,
        preferred_element_type=jnp.float32,
    ).astype(jnp.bfloat16)
    grad_attention = jnp.einsum(
        "rbqhe,rbkhe->rbhqk", grad_mixed, value_rows, preferred_element_type=jnp.float32
    )
    row_inner = jnp.sum(attention * grad_attention, -1, keepdims=True)
    grad_scores = (attention * (grad_attention - row_inner)).astype(jnp.bfloat16)
    grad_query = (
        jnp.einsum("rbhqk,rbkhe->rbqhe", grad_scores, key_rows, preferred_element_type=jnp.float32)
        * HEAD_DIM ** (-0.5)
    ).astype(jnp.bfloat16)
    grad_keys = (
        jnp.einsum(
            "rbhqk,rbqhe->rbkhe", grad_scores, query_rows, preferred_element_type=jnp.float32
        )
        * HEAD_DIM ** (-0.5)
    ).astype(jnp.bfloat16)
    return (grad_query, grad_keys, grad_values)


def per_device(
    image_tokens,
    caption_embed,
    caption_lengths,
    output_grad,
    norm_self,
    norm_cross,
    norm_feed,
    self_query,
    self_key,
    self_value,
    self_output,
    cross_query,
    cross_key,
    cross_value,
    cross_output,
    up_weight,
    down_weight,
):
    gathered = (
        lax.all_gather(norm_self, "rows", axis=0, tiled=True),
        lax.all_gather(norm_cross, "rows", axis=0, tiled=True),
        lax.all_gather(norm_feed, "rows", axis=0, tiled=True),
        lax.all_gather(self_query, "rows", axis=0, tiled=True),
        lax.all_gather(self_key, "rows", axis=0, tiled=True),
        lax.all_gather(self_value, "rows", axis=0, tiled=True),
        lax.all_gather(self_output, "rows", axis=1, tiled=True),
        lax.all_gather(cross_query, "rows", axis=0, tiled=True),
        lax.all_gather(cross_key, "rows", axis=0, tiled=True),
        lax.all_gather(cross_value, "rows", axis=0, tiled=True),
        lax.all_gather(cross_output, "rows", axis=1, tiled=True),
        lax.all_gather(up_weight, "rows", axis=0, tiled=True),
        lax.all_gather(down_weight, "rows", axis=1, tiled=True),
    )
    gain_one = gathered[0].astype(jnp.float32)
    gain_two = gathered[1].astype(jnp.float32)
    gain_three = gathered[2].astype(jnp.float32)
    residual = image_tokens.astype(jnp.float32)
    normed_one, inverse_one = layer_stats(residual)
    first_input_tensor = gather_tokens((normed_one * gain_one).astype(jnp.bfloat16))
    query_one = split_heads(project(first_input_tensor, gathered[3]), IMAGE_TOKENS)
    key_one = split_heads(project(first_input_tensor, gathered[4]), IMAGE_TOKENS)
    value_one = split_heads(project(first_input_tensor, gathered[5]), IMAGE_TOKENS)
    mixed_one, logsum_one = attend_forward(query_one, key_one, value_one, None)
    merged_one = join_heads(mixed_one)
    residual_two = residual + sum_tokens(product(merged_one, gathered[6]))
    normed_two, inverse_two = layer_stats(residual_two)
    input_two = gather_tokens((normed_two * gain_two).astype(jnp.bfloat16))
    caption_full = lax.all_gather(caption_embed, "text", axis=1, tiled=True)
    query_two = split_heads(project(input_two, gathered[7]), IMAGE_TOKENS)
    key_two = split_heads(project(caption_full, gathered[8]), CAP)
    value_two = split_heads(project(caption_full, gathered[9]), CAP)
    slot_index = lax.broadcasted_iota(jnp.int32, (1, 1, CAP), 2)
    live_slots = (slot_index < caption_lengths[:, :, None])[:, :, None, None, :]
    mixed_two, logsum_two = attend_forward(query_two, key_two, value_two, live_slots)
    merged_two = join_heads(mixed_two)
    residual_three = residual_two + sum_tokens(product(merged_two, gathered[10]))
    normed_three, inverse_three = layer_stats(residual_three)
    input_three = gather_tokens((normed_three * gain_three).astype(jnp.bfloat16))
    hidden_pre = product(input_three, gathered[11])
    hidden_act = jax.nn.gelu(hidden_pre, approximate=False).astype(jnp.bfloat16)
    block_out = residual_three + sum_tokens(product(hidden_act, gathered[12]))
    grad_resid = output_grad.astype(jnp.float32)
    grad_full = gather_grads(grad_resid.astype(jnp.bfloat16))
    grad_down = contract_product(hidden_act, grad_full)
    grad_act = jnp.einsum(
        "rsd,fd->rsf", grad_full, gathered[12], preferred_element_type=jnp.float32
    )
    grad_pre = gelu_back(hidden_pre, grad_act).astype(jnp.bfloat16)
    grad_up = contract_product(input_three, grad_pre)
    grad_norm = sum_inputs(product_back(grad_pre, gathered[11]))
    grad_input, feed_gain_grad = norm_back(grad_norm, normed_three, inverse_three, gain_three)
    grad_resid = grad_resid + grad_input
    grad_full = gather_grads(grad_resid.astype(jnp.bfloat16))
    grad_cout = contract_product(merged_two, grad_full)
    grad_merged = jnp.einsum(
        "rsd,ed->rse", grad_full, gathered[10], preferred_element_type=jnp.float32
    ).astype(jnp.bfloat16)
    cross_gq, cross_gk, cross_gv = attend_back(
        query_two,
        key_two,
        value_two,
        live_slots,
        logsum_two,
        split_heads(grad_merged, IMAGE_TOKENS),
    )
    cross_gq = join_heads(cross_gq)
    cross_gk = join_heads(cross_gk)
    cross_gv = join_heads(cross_gv)
    grad_cquery = contract_product(input_two, cross_gq)
    grad_ckey = contract_product(caption_full, cross_gk)
    grad_cvalue = contract_product(caption_full, cross_gv)
    caption_grad = lax.psum_scatter(
        (product_back(cross_gk, gathered[8]) + product_back(cross_gv, gathered[9])).astype(
            jnp.bfloat16
        ),
        "text",
        scatter_dimension=1,
        tiled=True,
    ).astype(jnp.float32)
    grad_norm = sum_inputs(product_back(cross_gq, gathered[7]))
    grad_input, cross_gain_grad = norm_back(grad_norm, normed_two, inverse_two, gain_two)
    grad_resid = grad_resid + grad_input
    grad_full = gather_grads(grad_resid.astype(jnp.bfloat16))
    grad_sout = contract_product(merged_one, grad_full)
    grad_merged = jnp.einsum(
        "rsd,ed->rse", grad_full, gathered[6], preferred_element_type=jnp.float32
    ).astype(jnp.bfloat16)
    self_gq, self_key_gradient_part, self_gv = attend_back(
        query_one, key_one, value_one, None, logsum_one, split_heads(grad_merged, IMAGE_TOKENS)
    )
    self_gq = join_heads(self_gq)
    self_key_gradient_part = join_heads(self_key_gradient_part)
    self_gv = join_heads(self_gv)
    grad_squery = contract_product(first_input_tensor, self_gq)
    self_attention_key_gradient = contract_product(first_input_tensor, self_key_gradient_part)
    grad_svalue = contract_product(first_input_tensor, self_gv)
    grad_norm = sum_inputs(
        product_back(self_gq, gathered[3])
        + product_back(self_key_gradient_part, gathered[4])
        + product_back(self_gv, gathered[5])
    )
    grad_input, self_norm_gain_gradient = norm_back(grad_norm, normed_one, inverse_one, gain_one)
    grad_resid = grad_resid + grad_input
    gain_totals = lax.psum((self_norm_gain_gradient, cross_gain_grad, feed_gain_grad), "text")
    results = (
        lax.psum_scatter(
            gain_totals[0].astype(jnp.bfloat16), "rows", scatter_dimension=0, tiled=True
        ).astype(jnp.float32),
        lax.psum_scatter(
            gain_totals[1].astype(jnp.bfloat16), "rows", scatter_dimension=0, tiled=True
        ).astype(jnp.float32),
        lax.psum_scatter(
            gain_totals[2].astype(jnp.bfloat16), "rows", scatter_dimension=0, tiled=True
        ).astype(jnp.float32),
        lax.psum_scatter(
            grad_squery.astype(jnp.bfloat16), "rows", scatter_dimension=0, tiled=True
        ).astype(jnp.float32),
        lax.psum_scatter(
            self_attention_key_gradient.astype(jnp.bfloat16),
            "rows",
            scatter_dimension=0,
            tiled=True,
        ).astype(jnp.float32),
        lax.psum_scatter(
            grad_svalue.astype(jnp.bfloat16), "rows", scatter_dimension=0, tiled=True
        ).astype(jnp.float32),
        lax.psum_scatter(
            grad_sout.astype(jnp.bfloat16), "rows", scatter_dimension=1, tiled=True
        ).astype(jnp.float32),
        lax.psum_scatter(
            grad_cquery.astype(jnp.bfloat16), "rows", scatter_dimension=0, tiled=True
        ).astype(jnp.float32),
        lax.psum_scatter(
            grad_ckey.astype(jnp.bfloat16), "rows", scatter_dimension=0, tiled=True
        ).astype(jnp.float32),
        lax.psum_scatter(
            grad_cvalue.astype(jnp.bfloat16), "rows", scatter_dimension=0, tiled=True
        ).astype(jnp.float32),
        lax.psum_scatter(
            grad_cout.astype(jnp.bfloat16), "rows", scatter_dimension=1, tiled=True
        ).astype(jnp.float32),
        lax.psum_scatter(
            grad_up.astype(jnp.bfloat16), "rows", scatter_dimension=0, tiled=True
        ).astype(jnp.float32),
        lax.psum_scatter(
            grad_down.astype(jnp.bfloat16), "rows", scatter_dimension=1, tiled=True
        ).astype(jnp.float32),
    )
    return (
        block_out.astype(jnp.bfloat16),
        grad_resid,
        caption_grad,
        results[0],
        results[1],
        results[2],
        results[3],
        results[4],
        results[5],
        results[6],
        results[7],
        results[8],
        results[9],
        results[10],
        results[11],
        results[12],
    )


def solution(mesh):
    in_specs = (
        P("rows", "text", None),
        P("rows", "text", None),
        P("rows", None),
        P("rows", "text", None),
        P("rows"),
        P("rows"),
        P("rows"),
        P("rows", "text"),
        P("rows", "text"),
        P("rows", "text"),
        P("text", "rows"),
        P("rows", "text"),
        P("rows", "text"),
        P("rows", "text"),
        P("text", "rows"),
        P("rows", "text"),
        P("text", "rows"),
    )
    out_specs = (
        P("rows", "text", None),
        P("rows", "text", None),
        P("rows", "text", None),
        P("rows"),
        P("rows"),
        P("rows"),
        P("rows", "text"),
        P("rows", "text"),
        P("rows", "text"),
        P("text", "rows"),
        P("rows", "text"),
        P("rows", "text"),
        P("rows", "text"),
        P("text", "rows"),
        P("rows", "text"),
        P("text", "rows"),
    )
    return jax.shard_map(
        per_device, mesh=mesh, in_specs=in_specs, out_specs=out_specs, check_vma=False
    )
```

profile of v0, /device:TPU:1, one launch (start us, length us, event | category | flops | bytes accessed | tf_op | source)
XLA Modules:
  0.0 3384.0 jit_solution(11320915709437666502)
XLA Ops:
  14.3 158.3 %all-reduce.8 = (bf16[2048]{0:T(1024)(128)(2,1)S(1)}, bf16[2048]{0:T(1024)(128)(2,1)S(1)}, bf16[2048]{0:T(1024)(128)(2,1)}) all-reduce(bf16[2048]{0:T(1024)(128)(2,1)S(1)} %dynamic-update-slice, bf16[2048]{0:T(1024)(128)(2,1)S(1)} %dynamic-update-slice.1, ...), channel_id=1, replica_groups=mesh['rows'=32,'text'=4] {'rows'}, use_global_device_ids=true, to_apply=%add | all-reduce | flops 6144 | bytes 24576
  177.6 49.1 %all-gather.17.cloned.1.call-done = bf16[1,512,2048]{2,1,0:T(8,128)(2,1)} async-done(((bf16[1,128,2048]{2,1,0:T(8,128)(2,1)}), bf16[1,512,2048]{2,1,0:T(8,128)(2,1)}) %all-gather.17.cloned.1.call-update) | async-done | bytes 2097168 | tf_op jit(solution)/shard_map/all_gather | solution.py:38
  226.6 72.9 %all-gather.21.cloned.1.call-done = bf16[2048,512]{1,0:T(8,128)(2,1)} async-done(((bf16[64,512]{1,0:T(8,128)(2,1)}), bf16[2048,512]{1,0:T(8,128)(2,1)}) %all-gather.21.cloned.1.call-update) | async-done | bytes 2097168 | tf_op jit(solution)/shard_map/all_gather | solution.py:154
  303.5 68.2 %all-gather.23.cloned.1.call-done = bf16[2048,512]{1,0:T(8,128)(2,1)} async-done(((bf16[64,512]{1,0:T(8,128)(2,1)}), bf16[2048,512]{1,0:T(8,128)(2,1)}) %all-gather.23.cloned.1.call-update) | async-done | bytes 2097168 | tf_op jit(solution)/shard_map/all_gather | solution.py:155
  375.6 68.1 %all-gather.19.cloned.1.call-done = bf16[2048,512]{1,0:T(8,128)(2,1)} async-done(((bf16[64,512]{1,0:T(8,128)(2,1)}), bf16[2048,512]{1,0:T(8,128)(2,1)}) %all-gather.19.cloned.1.call-update) | async-done | bytes 2097168 | tf_op jit(solution)/shard_map/all_gather | solution.py:156
  450.7 65.0 %all-gather.25.cloned.1.call-done = bf16[512,2048]{0,1:T(8,128)(2,1)} async-done(((bf16[512,64]{0,1:T(8,128)(2,1)}), bf16[512,2048]{0,1:T(8,128)(2,1)}) %all-gather.25.cloned.1.call-update) | async-done | bytes 2097168 | tf_op jit(solution)/shard_map/all_gather | solution.py:157
  522.8 43.1 %reduce-scatter.22.cloned.1.call-done = f32[1,128,2048]{2,1,0:T(8,128)} async-done(((f32[1,512,2048]{2,1,0:T(8,128)}), f32[1,128,2048]{2,1,0:T(8,128)}) %reduce-scatter.22.cloned.1.call-update) | async-done | bytes 1048592 | tf_op jit(solution)/shard_map/reduce_scatter | solution.py:42
  575.9 74.4 %all-gather.33.cloned.1.call-done = bf16[4096,512]{1,0:T(8,128)(2,1)} async-done(((bf16[128,512]{1,0:T(8,128)(2,1)}), bf16[4096,512]{1,0:T(8,128)(2,1)}) %all-gather.33.cloned.1.call-update) | async-done | bytes 4194320 | tf_op jit(solution)/shard_map/all_gather | solution.py:159
  653.9 79.3 %all-gather.27.cloned.1.call-done = bf16[4096,512]{1,0:T(8,128)(2,1)} async-done(((bf16[128,512]{1,0:T(8,128)(2,1)}), bf16[4096,512]{1,0:T(8,128)(2,1)}) %all-gather.27.cloned.1.call-update) | async-done | bytes 4194320 | tf_op jit(solution)/shard_map/all_gather | solution.py:160
  736.8 68.6 %all-gather.31.cloned.1.call-done = bf16[2048,512]{1,0:T(8,128)(2,1)} async-done(((bf16[64,512]{1,0:T(8,128)(2,1)}), bf16[2048,512]{1,0:T(8,128)(2,1)}) %all-gather.31.cloned.1.call-update) | async-done | bytes 2097168 | tf_op jit(solution)/shard_map/all_gather | solution.py:158
  805.4 31.4 all-gather.29.cloned.1.call-done
  849.6 60.7 %all-gather.35.cloned.1.call-done = bf16[512,2048]{0,1:T(8,128)(2,1)} async-done(((bf16[512,64]{0,1:T(8,128)(2,1)}), bf16[512,2048]{0,1:T(8,128)(2,1)}) %all-gather.35.cloned.1.call-update) | async-done | bytes 2097168 | tf_op jit(solution)/shard_map/all_gather | solution.py:161
  916.8 43.9 %reduce-scatter.24.cloned.1.call-done = f32[1,128,2048]{2,1,0:T(8,128)} async-done(((f32[1,512,2048]{2,1,0:T(8,128)}), f32[1,128,2048]{2,1,0:T(8,128)}) %reduce-scatter.24.cloned.1.call-update) | async-done | bytes 1048592 | tf_op jit(solution)/shard_map/reduce_scatter | solution.py:42
  965.9 102.1 %all-gather.39.cloned.1.call-done = bf16[2048,2048]{1,0:T(8,128)(2,1)} async-done(((bf16[64,2048]{1,0:T(8,128)(2,1)}), bf16[2048,2048]{1,0:T(8,128)(2,1)}) %all-gather.39.cloned.1.call-update) | async-done | bytes 8388624 | tf_op jit(solution)/shard_map/all_gather | solution.py:162
  1068.0 30.0 all-gather.37.cloned.1.call-done
  1098.0 18.3 multiply_convert_fusion
  1129.5 106.9 %all-gather.41.cloned.1.call-done = bf16[2048,2048]{0,1:T(8,128)(2,1)} async-done(((bf16[2048,64]{0,1:T(8,128)(2,1)}), bf16[2048,2048]{0,1:T(8,128)(2,1)}) %all-gather.41.cloned.1.call-update) | async-done | bytes 8388624 | tf_op jit(solution)/shard_map/all_gather | solution.py:163
  1266.7 16.3 reduce-scatter.28.cloned.1.call-done
  1286.0 45.8 %reduce-scatter.26.cloned.1.call-done = f32[1,128,2048]{2,1,0:T(8,128)} async-done(((f32[1,512,2048]{2,1,0:T(8,128)}), f32[1,128,2048]{2,1,0:T(8,128)}) %reduce-scatter.26.cloned.1.call-update) | async-done | bytes 1048592 | tf_op jit(solution)/shard_map/reduce_scatter | solution.py:42
  1336.5 29.6 all-gather.45.cloned.1.call-done
  1383.5 29.0 reduce-scatter.30.cloned.1.call-done
  1520.2 114.4 %reduce-scatter.46.cloned.1.call-done = bf16[512,64]{0,1:T(8,128)(2,1)} async-done(((bf16[512,2048]{0,1:T(8,128)(2,1)}), bf16[512,64]{0,1:T(8,128)(2,1)}) %reduce-scatter.46.cloned.1.call-update) | async-done | bytes 65552 | tf_op jit(solution)/shard_map/reduce_scatter | solution.py:290
  1636.1 183.5 %reduce-scatter.44.cloned.1.call-done = bf16[64,512]{1,0:T(8,128)(2,1)} async-done(((bf16[2048,512]{1,0:T(8,128)(2,1)}), bf16[64,512]{1,0:T(8,128)(2,1)}) %reduce-scatter.44.cloned.1.call-update) | async-done | bytes 65552 | tf_op jit(solution)/shard_map/reduce_scatter | solution.py:281
  1821.1 199.0 %reduce-scatter.50.cloned.1.call-done = bf16[2048,64]{0,1:T(8,128)(2,1)} async-done(((bf16[2048,2048]{0,1:T(8,128)(2,1)}), bf16[2048,64]{0,1:T(8,128)(2,1)}) %reduce-scatter.50.cloned.1.call-update) | async-done | bytes 262160 | tf_op jit(solution)/shard_map/reduce_scatter | solution.py:296
  2021.9 198.3 %reduce-scatter.48.cloned.1.call-done = bf16[64,2048]{1,0:T(8,128)(2,1)} async-done(((bf16[2048,2048]{1,0:T(8,128)(2,1)}), bf16[64,2048]{1,0:T(8,128)(2,1)}) %reduce-scatter.48.cloned.1.call-update) | async-done | bytes 262160 | tf_op jit(solution)/shard_map/reduce_scatter | solution.py:293
  2222.0 188.3 %reduce-scatter.54.cloned.1.call-done = bf16[128,512]{1,0:T(8,128)(2,1)} async-done(((bf16[4096,512]{1,0:T(8,128)(2,1)}), bf16[128,512]{1,0:T(8,128)(2,1)}) %reduce-scatter.54.cloned.1.call-update) | async-done | bytes 131088
  2412.1 187.5 %reduce-scatter.52.cloned.1.call-done = bf16[128,512]{1,0:T(8,128)(2,1)} async-done(((bf16[4096,512]{1,0:T(8,128)(2,1)}), bf16[128,512]{1,0:T(8,128)(2,1)}) %reduce-scatter.52.cloned.1.call-update) | async-done | bytes 131088
  2601.4 180.8 %reduce-scatter.42.cloned.1.call-done = bf16[512,64]{0,1:T(8,128)(2,1)} async-done(((bf16[512,2048]{0,1:T(8,128)(2,1)}), bf16[512,64]{0,1:T(8,128)(2,1)}) %reduce-scatter.42.cloned.1.call-update) | async-done | bytes 65552 | tf_op jit(solution)/shard_map/reduce_scatter | solution.py:278
  2783.7 184.1 %reduce-scatter.38.cloned.1.call-done = bf16[64,512]{1,0:T(8,128)(2,1)} async-done(((bf16[2048,512]{1,0:T(8,128)(2,1)}), bf16[64,512]{1,0:T(8,128)(2,1)}) %reduce-scatter.38.cloned.1.call-update) | async-done | bytes 65552 | tf_op jit(solution)/shard_map/reduce_scatter | solution.py:269
  2969.3 181.3 %reduce-scatter.36.cloned.1.call-done = bf16[64,512]{1,0:T(8,128)(2,1)} async-done(((bf16[2048,512]{1,0:T(8,128)(2,1)}), bf16[64,512]{1,0:T(8,128)(2,1)}) %reduce-scatter.36.cloned.1.call-update) | async-done | bytes 65552 | tf_op jit(solution)/shard_map/reduce_scatter | solution.py:266
  3152.1 48.9 %reduce-scatter.32.cloned.1.call-done = bf16[1,128,2048]{2,1,0:T(8,128)(2,1)} async-done(((bf16[1,512,2048]{2,1,0:T(8,128)(2,1)}), bf16[1,128,2048]{2,1,0:T(8,128)(2,1)}) %reduce-scatter.32.cloned.1.call-update) | async-done | bytes 524304 | tf_op jit(solution)/shard_map/reduce_scatter | solution.py:50
  3212.8 158.1 %all-reduce.7 = (bf16[2048]{0:T(1024)(128)(2,1)S(1)}, bf16[2048]{0:T(1024)(128)(2,1)S(1)}, bf16[2048]{0:T(1024)(128)(2,1)S(1)}) all-reduce(bf16[2048]{0:T(1024)(128)(2,1)S(1)} %get-tuple-element.73, bf16[2048]{0:T(1024)(128)(2,1)S(1)} %get-tuple-element.74, ...), channel_id=9, replica_groups=mesh['rows'=32,'text'=4] {'rows'}, use_global_device_ids=true, to_apply=%region_27.28.clone | all-reduce | flops 6144 | bytes 24576
  (287 shorter events, 281.8 us)
Async XLA Ops:
  7.2 219.5 %all-gather.17.cloned.1.call-start = ((), (), s32[]{:S(2)}) async-start(), calls=%async_computation.17 | async-start | bytes 2621440 | tf_op jit(solution)/shard_map/all_gather | solution.py:38
  174.9 124.7 %all-gather.21.cloned.1.call-start = ((), (), s32[]{:S(2)}) async-start(), calls=%async_computation.19 | async-start | bytes 2162688 | tf_op jit(solution)/shard_map/all_gather | solution.py:154
  175.6 196.1 %all-gather.23.cloned.1.call-start = ((), (), s32[]{:S(2)}) async-start(), calls=%async_computation.20 | async-start | bytes 2162688 | tf_op jit(solution)/shard_map/all_gather | solution.py:155
  176.4 267.3 %all-gather.19.cloned.1.call-start = ((), (), s32[]{:S(2)}) async-start(), calls=%async_computation.18 | async-start | bytes 2162688 | tf_op jit(solution)/shard_map/all_gather | solution.py:156
  176.9 338.7 %all-gather.25.cloned.1.call-start = ((), (), s32[]{:S(2)}) async-start(), calls=%async_computation.21 | async-start | bytes 2162688 | tf_op jit(solution)/shard_map/all_gather | solution.py:157
  177.5 388.4 %reduce-scatter.22.cloned.1.call-start = ((), (), s32[]{:S(2)}) async-start(), calls=%async_computation.22 | async-start | bytes 5242880 | tf_op jit(solution)/shard_map/reduce_scatter | solution.py:42
  520.5 129.7 %all-gather.33.cloned.1.call-start = ((), (), s32[]{:S(2)}) async-start(), calls=%async_computation.26 | async-start | bytes 4325376 | tf_op jit(solution)/shard_map/all_gather | solution.py:159
  521.3 211.9 %all-gather.27.cloned.1.call-start = ((), (), s32[]{:S(2)}) async-start(), calls=%async_computation.23 | async-start | bytes 4325376 | tf_op jit(solution)/shard_map/all_gather | solution.py:160
  522.0 283.4 %all-gather.31.cloned.1.call-start = ((), (), s32[]{:S(2)}) async-start(), calls=%async_computation.25 | async-start | bytes 2162688 | tf_op jit(solution)/shard_map/all_gather | solution.py:158
  522.8 314.0 %all-gather.29.cloned.1.call-start = ((), (), s32[]{:S(2)}) async-start(), calls=%async_computation.24 | async-start | bytes 2621440 | tf_op jit(solution)/shard_map/all_gather | solution.py:38
  568.8 341.5 %all-gather.35.cloned.1.call-start = ((), (), s32[]{:S(2)}) async-start(), calls=%async_computation.27 | async-start | bytes 2162688 | tf_op jit(solution)/shard_map/all_gather | solution.py:161
  569.5 391.2 %reduce-scatter.24.cloned.1.call-start = ((), (), s32[]{:S(2)}) async-start(), calls=%async_computation.28 | async-start | bytes 5242880 | tf_op jit(solution)/shard_map/reduce_scatter | solution.py:42
  915.3 152.7 %all-gather.39.cloned.1.call-start = ((), (), s32[]{:S(2)}) async-start(), calls=%async_computation.30 | async-start | bytes 8650752 | tf_op jit(solution)/shard_map/all_gather | solution.py:162
  916.1 181.9 %all-gather.37.cloned.1.call-start = ((), (), s32[]{:S(2)}) async-start(), calls=%async_computation.29 | async-start | bytes 2621440 | tf_op jit(solution)/shard_map/all_gather | solution.py:38
  964.7 164.9 %all-gather.43.cloned.1.call-start = ((), (), s32[]{:S(2)}) async-start(), calls=%async_computation.33 | async-start | bytes 2621440 | tf_op jit(solution)/shard_map/all_gather | solution.py:46
  965.2 271.2 %all-gather.41.cloned.1.call-start = ((), (), s32[]{:S(2)}) async-start(), calls=%async_computation.31 | async-start | bytes 8650752 | tf_op jit(solution)/shard_map/all_gather | solution.py:163
  965.8 317.3 %reduce-scatter.28.cloned.1.call-start = ((), (), s32[]{:S(2)}) async-start(), calls=%async_computation.34 | async-start | bytes 2621440 | tf_op jit(solution)/shard_map/reduce_scatter | solution.py:50
  1266.7 99.4 %all-gather.45.cloned.1.call-start = ((), (), s32[]{:S(2)}) async-start(), calls=%async_computation.35 | async-start | bytes 2621440 | tf_op jit(solution)/shard_map/all_gather | solution.py:46
  1335.7 76.8 %reduce-scatter.30.cloned.1.call-start = ((), (), s32[]{:S(2)}) async-start(), calls=%async_computation.36 | async-start | bytes 2621440 | tf_op jit(solution)/shard_map/reduce_scatter | solution.py:50
  1383.4 92.7 %all-gather.47.cloned.1.call-start = ((), (), s32[]{:S(2)}) async-start(), calls=%async_computation.37 | async-start | bytes 2621440 | tf_op jit(solution)/shard_map/all_gather | solution.py:46
  1417.6 101.1 %reduce-scatter.34.cloned.1.call-start = ((), (), s32[]{:S(2)}) async-start(), calls=%async_computation.39 | async-start | bytes 327680 | tf_op jit(solution)/shard_map/reduce_scatter | solution.py:223
  1426.2 208.3 %reduce-scatter.46.cloned.1.call-start = ((), (), s32[]{:S(2)}) async-start(), calls=%async_computation.45 | async-start | bytes 2162688 | tf_op jit(solution)/shard_map/reduce_scatter | solution.py:290
  1430.7 388.9 %reduce-scatter.44.cloned.1.call-start = ((), (), s32[]{:S(2)}) async-start(), calls=%async_computation.44 | async-start | bytes 2162688 | tf_op jit(solution)/shard_map/reduce_scatter | solution.py:281
  1435.0 585.1 %reduce-scatter.50.cloned.1.call-start = ((), (), s32[]{:S(2)}) async-start(), calls=%async_computation.47 | async-start | bytes 8650752 | tf_op jit(solution)/shard_map/reduce_scatter | solution.py:296
  1445.2 775.0 %reduce-scatter.48.cloned.1.call-start = ((), (), s32[]{:S(2)}) async-start(), calls=%async_computation.46 | async-start | bytes 8650752 | tf_op jit(solution)/shard_map/reduce_scatter | solution.py:293
  1455.5 954.8 %reduce-scatter.54.cloned.1.call-start = ((), (), s32[]{:S(2)}) async-start(), calls=%async_computation.49 | async-start | bytes 4325376
  1465.4 1134.2 %reduce-scatter.52.cloned.1.call-start = ((), (), s32[]{:S(2)}) async-start(), calls=%async_computation.48 | async-start | bytes 4325376
  1476.1 1306.2 %reduce-scatter.42.cloned.1.call-start = ((), (), s32[]{:S(2)}) async-start(), calls=%async_computation.43 | async-start | bytes 2162688 | tf_op jit(solution)/shard_map/reduce_scatter | solution.py:278
  1481.3 1486.5 %reduce-scatter.38.cloned.1.call-start = ((), (), s32[]{:S(2)}) async-start(), calls=%async_computation.41 | async-start | bytes 2162688 | tf_op jit(solution)/shard_map/reduce_scatter | solution.py:269
  1496.4 1654.2 %reduce-scatter.36.cloned.1.call-start = ((), (), s32[]{:S(2)}) async-start(), calls=%async_computation.40 | async-start | bytes 2162688 | tf_op jit(solution)/shard_map/reduce_scatter | solution.py:266
  1505.1 1695.9 %reduce-scatter.32.cloned.1.call-start = ((), (), s32[]{:S(2)}) async-start(), calls=%async_computation.38 | async-start | bytes 2621440 | tf_op jit(solution)/shard_map/reduce_scatter | solution.py:50
  1515.2 1857.5 %reduce-scatter.40.cloned.1.call-start = ((), (), s32[]{:S(2)}) async-start(), calls=%async_computation.42 | async-start | bytes 2162688 | tf_op jit(solution)/shard_map/reduce_scatter | solution.py:275
  (48 other events, 13602.6 us)
Sparse Core Ops, SparseCore 0:
  175.0 51.5 all-gather.16
  229.8 69.7 all-gather.20
  302.8 68.8 all-gather.22
  374.7 68.9 all-gather.18
  446.7 68.9 all-gather.24
  520.6 45.2 reduce-scatter.21
  569.5 80.6 all-gather.32
  653.9 79.2 all-gather.26
  736.8 68.5 all-gather.30
  807.6 29.1 all-gather.28
  840.5 69.7 all-gather.34
  915.5 45.2 reduce-scatter.23
  963.9 104.0 all-gather.38
  1070.1 27.8 all-gather.36
  1099.5 29.9 all-gather.42
  1132.5 103.8 all-gather.40
  1256.2 26.8 reduce-scatter.27
  1285.5 46.2 reduce-scatter.25
  1335.8 30.2 all-gather.44
  1383.5 28.8 reduce-scatter.29
  1417.7 30.2 all-gather.46
  1471.6 162.9 reduce-scatter.45
  1636.9 182.6 reduce-scatter.43
  1822.0 198.0 reduce-scatter.49
  2022.4 197.7 reduce-scatter.47
  2222.4 187.8 reduce-scatter.53
  2412.7 186.8 reduce-scatter.51
  2602.0 180.2 reduce-scatter.41
  2784.6 183.1 reduce-scatter.37
  2970.2 180.3 reduce-scatter.35
  3153.1 47.8 reduce-scatter.31
  3203.2 164.1 reduce-scatter.39
  (1 shorter events, 18.1 us)
where the time goes:
time: 3420 us; the launch traced here: 3380 us
  waiting for transfers between devices  2770 us (81%)
  blocking collectives  333 us (10%)
  matrix products  169 us (5%)
  local copies, waits for them, and re-layouts  47 us (1%)
  other arithmetic  45.3 us (1%)
    unnamed x35, waiting for transfers between devices  383 us
    unnamed x2, blocking collectives  316 us
    reduce_scatter x1, waiting for transfers between devices, per_device(): lax.psum_scatter(grad_down.astype(jnp.bfloat16), 'rows', scatter_dimensio...  199 us
    reduce_scatter x1, waiting for transfers between devices, per_device(): lax.psum_scatter(grad_up.astype(jnp.bfloat16), 'rows', scatter_dimension=...  198 us
    reduce_scatter x1, waiting for transfers between devices, per_device(): lax.psum_scatter(self_attention_key_gradient.astype(jnp.bfloat16), 'rows'...  184 us
    reduce_scatter x1, waiting for transfers between devices, per_device(): lax.psum_scatter(grad_cquery.astype(jnp.bfloat16), 'rows', scatter_dimens...  184 us
    reduce_scatter x1, waiting for transfers between devices, per_device(): lax.psum_scatter(grad_squery.astype(jnp.bfloat16), 'rows', scatter_dimens...  181 us
    reduce_scatter x1, waiting for transfers between devices, per_device(): lax.psum_scatter(grad_sout.astype(jnp.bfloat16), 'rows', scatter_dimensio...  181 us
  transfers between devices with their start and end apart: 33, of which 30 were waited for; matrix products, arithmetic and copies ran while one was open for 6% of the time, Pallas kernels for 0%

commit v1 on v0

v1 whole, which is shorter than its diff:
```python
import jax
import jax.numpy as jnp
from jax import lax
from jax.sharding import Mesh, PartitionSpec as P

HEAD = 128
CAP = 16
EPSILON = 1e-05
SCALE = HEAD ** (-0.5)
BF = jnp.bfloat16
F32 = jnp.float32
RING = ("xh", "xl")
PLANE = ("y", "z")


def px(value, step):
    return lax.ppermute(value, RING, [(i, (i + step) % 4) for i in range(4)])


def swap(value, axis):
    return lax.ppermute(value, axis, [(0, 1), (1, 0)])


def dot(a, b, ca, cb, out=F32):
    return lax.dot_general(a, b, (((ca,), (cb,)), ((), ())), preferred_element_type=F32).astype(out)


def gather_tokens(part):
    half = part.shape[0] // 2
    left, right = px(part, 1), px(part, -1)
    far = jnp.concatenate([px(left[:half], 1), px(right[half:], -1)], 0)
    pieces = []
    for piece in (part, left, right, far):
        pieces += [piece, swap(piece, "c")]
    return jnp.concatenate(pieces, 0)


def scatter_tokens(partial):
    parts = partial.reshape(4, 2, partial.shape[0] // 8, partial.shape[1])
    other = swap(parts[:, 1], "c")
    total = parts[:, 0].astype(F32) + other.astype(F32)
    low = total.astype(BF)
    a, b, c = px(low[1], -1), px(low[2], 1), px(low[3], 2)
    return total[0] + a.astype(F32) + b.astype(F32) + c.astype(F32)


def stats(resid):
    mean = jnp.mean(resid, -1, keepdims=True)
    centered = resid - mean
    inverse = lax.rsqrt(jnp.mean(centered * centered, -1, keepdims=True) + EPSILON)
    return centered * inverse, inverse


def norm_back(grad, normed, inverse, gain):
    scaled = grad * gain
    inner = (
        scaled
        - jnp.mean(scaled, -1, keepdims=True)
        - normed * jnp.mean(scaled * normed, -1, keepdims=True)
    )
    return inverse * inner, jnp.sum(grad * normed, axis=0)


def gelu_back(pre, grad):
    _, pullback = jax.vjp(lambda v: jax.nn.gelu(v, approximate=False), pre)
    return pullback(grad)[0]


def mix_features(value):
    n = value.shape[0]
    return value.reshape(n, 2, 16, 64).transpose(0, 2, 1, 3).reshape(n, 2048)


def unmix_features(value):
    n = value.shape[0]
    return value.reshape(n, 16, 2, 64).transpose(0, 2, 1, 3).reshape(n, 2048)


def per_device(
    image_tokens,
    caption_embed,
    caption_lengths,
    output_grad,
    norm_self,
    norm_cross,
    norm_feed,
    self_query,
    self_key,
    self_value,
    self_output,
    cross_query,
    cross_key,
    cross_value,
    cross_output,
    up_weight,
    down_weight,
):
    xh = lax.axis_index("xh")
    xl = lax.axis_index("xl")
    core = lax.axis_index("c")

    def halves(weight):
        n = weight.shape[1] // 2
        first, second = weight[:, :n], weight[:, n:]
        return jnp.where(xh == 0, first, second), jnp.where(xh == 0, second, first)

    def in_order(mine, theirs):
        return jnp.where(xh == 0, mine, theirs), jnp.where(xh == 0, theirs, mine)

    def gather_weights(weights, extra=None):
        pairs = [halves(w) for w in weights]
        mine = [p[0] for p in pairs]
        send = [p[1] for p in pairs]
        if extra is not None:
            mine.append(extra)
            send.append(extra)
        mine = jnp.concatenate(mine, 1)
        theirs = swap(jnp.concatenate(send, 1), "xh")
        pair = jnp.concatenate(in_order(mine, theirs), 0)
        return lax.all_gather(pair, PLANE, axis=0, tiled=True)

    def scatter_grads(grads, widths):
        total = lax.psum_scatter(grads.astype(BF), PLANE, scatter_dimension=0, tiled=True)
        keep = jnp.where(xh == 0, total[:64], total[64:])
        send = jnp.where(xh == 0, total[64:], total[:64])
        theirs = swap(send, "xh")
        outs, at = [], 0
        for width in widths:
            outs.append(
                jnp.concatenate(
                    in_order(keep[:, at : at + width], theirs[:, at : at + width]), 1
                ).astype(F32)
            )
            at += width
        return outs

    gains = jnp.stack([norm_self, norm_cross, norm_feed], 1)
    gains = jnp.pad(gains, ((0, 0), (0, 125)))
    first = gather_weights((self_query, self_key, self_value), gains)
    qkv_weight = first[:, :768]
    gain = first[:, 768:771].astype(F32).T
    gain_one, gain_two, gain_three = gain[0:1], gain[1:2], gain[2:3]
    second = gather_weights(
        (
            self_output.T,
            cross_query,
            cross_output.T,
            cross_key[:64],
            cross_value[:64],
            cross_key[64:],
            cross_value[64:],
        )
    )
    out_weight = second[:, :256]
    cq_weight = second[:, 256:512]
    co_weight = second[:, 512:768]
    kv_weight = (second[:, 768:1280], second[:, 1280:1792])
    third = gather_weights((up_weight, down_weight.T))
    up, down = third[:, :1024], third[:, 1024:]

    resid = mix_features(image_tokens[0]).astype(F32)
    normed_one, inverse_one = stats(resid)
    grad_low = mix_features(output_grad[0])
    h1 = (gather_tokens(normed_one.astype(BF)).astype(F32) * gain_one).astype(BF)
    grad_full = gather_tokens(grad_low)

    caption = caption_embed[0].reshape(8, 2, 16, 2, 64).transpose(0, 3, 2, 1, 4).reshape(8, 4096)
    sibling = swap(caption, "c")
    caption = jnp.concatenate(
        [jnp.where(core == 0, caption, sibling), jnp.where(core == 0, sibling, caption)], 0
    )
    caption = jnp.concatenate([caption, px(caption, 1), px(caption, -1), px(caption, 2)], 0)
    cap_a, cap_b = caption[:, :2048], caption[:, 2048:]

    qkv = dot(h1, qkv_weight, 1, 0, BF)
    q1 = qkv[:, :256].reshape(4, 256, 2, HEAD)
    k1 = qkv[:, 256:512].reshape(4, 256, 2, HEAD)
    v1 = qkv[:, 512:].reshape(4, 256, 2, HEAD)
    scores = jnp.einsum("iqhe,ikhe->ihqk", q1, k1, preferred_element_type=F32) * SCALE
    shifted = jnp.exp(scores - jnp.max(scores, -1, keepdims=True))
    p1 = shifted / jnp.sum(shifted, -1, keepdims=True)
    o1 = jnp.einsum("ihqk,ikhe->iqhe", p1.astype(BF), v1, preferred_element_type=F32)
    o1 = o1.astype(BF).reshape(1024, 256)
    resid_two = resid + scatter_tokens(dot(o1, out_weight, 1, 1, BF))
    normed_two, inverse_two = stats(resid_two)
    h2 = (normed_two * gain_two).astype(BF)

    kv = (dot(cap_a, kv_weight[0], 1, 0) + dot(cap_b, kv_weight[1], 1, 0)).astype(BF)
    k2 = kv[:, :256].reshape(64, 2, HEAD)
    v2 = kv[:, 256:].reshape(64, 2, HEAD)
    cq_heads = cq_weight.reshape(2048, 2, HEAD)
    co_heads = co_weight.reshape(2048, 2, HEAD)
    m_part = jnp.einsum("she,dhe->hsd", k2, cq_heads, preferred_element_type=F32).astype(BF)
    n_part = jnp.einsum("she,dhe->hsd", v2, co_heads, preferred_element_type=F32).astype(BF)
    both = jnp.stack([m_part, n_part], 0).reshape(4, 4, CAP, 2048).transpose(1, 0, 2, 3)
    both = both.reshape(4, 64, 2048)
    got = jnp.stack([both[0], px(both[1], -1), px(both[2], 1), px(both[3], 2)], 0)
    got = jnp.stack([got, swap(got, "c")], 0).reshape(8, 2, 32, 2048)
    m_all = got[:, 0].reshape(256, 2048)
    n_all = got[:, 1].reshape(256, 2048)
    length = jnp.where(xl == 0, caption_lengths[0, 0], caption_lengths[0, 1])
    live = lax.broadcasted_iota(jnp.int32, (1, CAP, 1), 1) < length
    scores = dot(m_all, h2, 1, 1).reshape(16, CAP, 128) * SCALE
    scores = jnp.where(live, scores, -1e30)
    shifted = jnp.exp(scores - jnp.max(scores, 1, keepdims=True))
    p2 = shifted / jnp.sum(shifted, 1, keepdims=True)
    p2_low = p2.astype(BF).reshape(256, 128)
    resid_three = resid_two + dot(p2_low, n_all, 0, 0)
    normed_three, inverse_three = stats(resid_three)
    h3 = gather_tokens((normed_three * gain_three).astype(BF))

    hidden = dot(h3, up, 1, 0)
    act = jax.nn.gelu(hidden, approximate=False).astype(BF)
    grad_hidden = gelu_back(hidden, dot(grad_full, down, 1, 0)).astype(BF)
    grad_norm = scatter_tokens(dot(grad_hidden, up, 1, 1, BF))
    block_out = resid_three + scatter_tokens(dot(act, down, 1, 1, BF))
    up_grad = dot(h3, grad_hidden, 0, 0, BF)
    down_grad = dot(grad_full, act, 0, 0, BF)
    up_out, down_out = scatter_grads(jnp.concatenate([up_grad, down_grad], 1), (1024, 1024))
    grad_resid = grad_low.astype(F32)
    step, feed_gain = norm_back(grad_norm, normed_three, inverse_three, gain_three)
    grad_resid = grad_resid + step

    low = grad_resid.astype(BF)
    grad_p = dot(n_all, low, 1, 1).reshape(16, CAP, 128)
    grad_s = p2 * (grad_p - jnp.sum(p2 * grad_p, 1, keepdims=True))
    grad_s = grad_s.astype(BF).reshape(256, 128)
    grad_norm = dot(grad_s, m_all, 0, 0) * SCALE
    step, cross_gain = norm_back(grad_norm, normed_two, inverse_two, gain_two)
    grad_resid = grad_resid + step
    grad_m = (dot(grad_s, h2, 1, 0) * SCALE).astype(BF).reshape(8, 32, 2048)
    grad_n = dot(p2_low, low, 1, 0, BF).reshape(8, 32, 2048)
    back = jnp.concatenate([grad_m, grad_n], 1).reshape(2, 4, 64, 2048)
    back = (back[0].astype(F32) + swap(back[1], "c").astype(F32)).astype(BF)
    back = jnp.stack([back[0], px(back[1], 1), px(back[2], -1), px(back[3], 2)], 0)
    back = back.reshape(4, 2, 2, CAP, 2048).transpose(1, 2, 0, 3, 4).reshape(2, 2, 64, 2048)
    cq_grad = jnp.einsum("hsd,she->dhe", back[0], k2, preferred_element_type=F32)
    co_grad = jnp.einsum("hsd,she->dhe", back[1], v2, preferred_element_type=F32)
    grad_k = jnp.einsum("hsd,dhe->she", back[0], cq_heads, preferred_element_type=F32)
    grad_v = jnp.einsum("hsd,dhe->she", back[1], co_heads, preferred_element_type=F32)
    grad_kv = jnp.concatenate([grad_k.reshape(64, 256), grad_v.reshape(64, 256)], 1).astype(BF)
    kv_grad_a = dot(cap_a, grad_kv, 0, 0, BF)
    kv_grad_b = dot(cap_b, grad_kv, 0, 0, BF)
    cap_grad = jnp.concatenate(
        [dot(grad_kv, kv_weight[0], 1, 1), dot(grad_kv, kv_weight[1], 1, 1)], 1
    )
    cap_grad = cap_grad.astype(BF).reshape(4, 2, 8, 4096)
    keep = jnp.where(core == 0, cap_grad[:, 0], cap_grad[:, 1])
    send = jnp.where(core == 0, cap_grad[:, 1], cap_grad[:, 0])
    total = keep.astype(F32) + swap(send, "c").astype(F32)
    low_cap = total.astype(BF)
    cap_out = (
        total[0]
        + px(low_cap[1], -1).astype(F32)
        + px(low_cap[2], 1).astype(F32)
        + px(low_cap[3], 2).astype(F32)
    )
    cap_out = cap_out.reshape(8, 2, 16, 2, 64).transpose(0, 3, 2, 1, 4).reshape(1, 8, 4096)

    grad_full = gather_tokens(grad_resid.astype(BF))
    out_grad = dot(grad_full, o1, 0, 0, BF)
    go1 = dot(grad_full, out_weight, 1, 0, BF).reshape(4, 256, 2, HEAD)
    grad_v1 = jnp.einsum("ihqk,iqhe->ikhe", p1.astype(BF), go1, preferred_element_type=F32)
    grad_p = jnp.einsum("iqhe,ikhe->ihqk", go1, v1, preferred_element_type=F32)
    grad_s = (p1 * (grad_p - jnp.sum(p1 * grad_p, -1, keepdims=True))).astype(BF)
    grad_q1 = jnp.einsum("ihqk,ikhe->iqhe", grad_s, k1, preferred_element_type=F32) * SCALE
    grad_k1 = jnp.einsum("ihqk,iqhe->ikhe", grad_s, q1, preferred_element_type=F32) * SCALE
    grad_qkv = jnp.concatenate(
        [g.astype(BF).reshape(1024, 256) for g in (grad_q1, grad_k1, grad_v1)], 1
    )
    grad_norm = scatter_tokens(dot(grad_qkv, qkv_weight, 1, 1, BF))
    qkv_grad = dot(h1, grad_qkv, 0, 0, BF)
    step, self_gain = norm_back(grad_norm, normed_one, inverse_one, gain_one)
    image_grad = unmix_features(grad_resid + step)[None]

    rest = scatter_grads(
        jnp.concatenate(
            [
                qkv_grad,
                out_grad,
                cq_grad.reshape(2048, 256).astype(BF),
                co_grad.reshape(2048, 256).astype(BF),
                kv_grad_a,
                kv_grad_b,
            ],
            1,
        ),
        (256,) * 10,
    )

    terms = jnp.stack([self_gain, cross_gain, feed_gain], 0)
    terms = terms.reshape(3, 16, 128).transpose(1, 0, 2).reshape(16, 384)
    terms = lax.all_to_all(terms, PLANE, split_axis=0, concat_axis=0)
    terms = jnp.sum(terms.reshape(16, 3, 2, 64), 0)
    keep = jnp.where(xh == 0, terms[:, 0], terms[:, 1])
    keep = keep + swap(jnp.where(xh == 0, terms[:, 1], terms[:, 0]), "xh")
    keep = keep + swap(keep, "xl")
    keep = keep + swap(keep, "c")

    return (
        unmix_features(block_out.astype(BF))[None],
        image_grad,
        cap_out,
        keep[0],
        keep[1],
        keep[2],
        rest[0],
        rest[1],
        rest[2],
        rest[3].T,
        rest[4],
        jnp.concatenate([rest[6], rest[8]], 0),
        jnp.concatenate([rest[7], rest[9]], 0),
        rest[5].T,
        up_out,
        down_out.T,
    )


def solution(mesh):
    names = ("xh", "y", "z", "xl", "c")
    fine = Mesh(mesh.devices.reshape(2, 4, 4, 2, 2), names)
    rows, text = ("xh", "y", "z"), ("xl", "c")
    tokens = P(rows, text, None)
    by_row = P(rows, text)
    by_text = P(text, rows)
    in_specs = (
        (tokens, tokens, P(rows, None), tokens)
        + (P(rows),) * 3
        + (by_row, by_row, by_row, by_text)
        + (by_row, by_row, by_row, by_text)
        + (by_row, by_text)
    )
    out_specs = (
        (tokens,) * 3
        + (P(rows),) * 3
        + (by_row, by_row, by_row, by_text)
        + (by_row, by_row, by_row, by_text)
        + (by_row, by_text)
    )
    return jax.shard_map(
        per_device, mesh=fine, in_specs=in_specs, out_specs=out_specs, check_vma=False
    )
```

time: 3420 us -> 632 us (0.18)
  waiting for transfers between devices: 2770 us -> 210 us
  blocking collectives: 333 us -> 0 us
  starting transfers between devices: 1.97 us -> 119 us
  local copies, waits for them, and re-layouts: 47 us -> 117 us
  matrix products: 169 us -> 108 us
    reduce_scatter x15 -> x0, waiting for transfers between devices: 1470 us -> none  [the longest x1 199 us: per_device(): lax.psum_scatter(grad_down.astype(jnp.bfloat16), 'rows', scatter_dimensio...]
    all_gather x16 -> x3, waiting for transfers between devices: 919 us -> 33.3 us  [gather_weights(): return lax.all_gather(pair, PLANE, axis=0, tiled=True)]
    unnamed x35 -> x7, waiting for transfers between devices: 383 us -> 0.08 us
    unnamed x2 -> x0, blocking collectives: 316 us -> none
    ppermute x0 -> x72, waiting for transfers between devices: none -> 171 us  [the longest x40 139 us: px(): return lax.ppermute(value, RING, [(i, (i + step) % 4) for i in range(4)])]
    ppermute x0 -> x72, starting transfers between devices: none -> 114 us  [the longest x32 68.7 us: swap(): return lax.ppermute(value, axis, [(0, 1), (1, 0)])]
    dot_general x42 -> x34, matrix products: 169 us -> 104 us  [the longest x23 94.6 us: dot(): lax.dot_general(a, b, (((ca,), (cb,)), ((), ())), preferred_element_type=...]
    unnamed x107 -> x203, local copies, waits for them, and re-layouts: 28.7 us -> 70.6 us
  transfers between devices with their start and end apart: 33 -> 78, of which waited for: 30 -> 32; matrix products, arithmetic and copies ran while one was open for 6% -> 33% of each run, Pallas kernels for 0% -> 0%
where the time goes in v1:
time: 632 us; the launch traced here: 622 us
  waiting for transfers between devices  210 us (33%)
  starting transfers between devices  119 us (19%)
  local copies, waits for them, and re-layouts  117 us (19%)
  matrix products  108 us (17%)
  other arithmetic  51.6 us (8%)
  between operations  17.4 us (3%)
    ppermute x40, waiting for transfers between devices, px(): return lax.ppermute(value, RING, [(i, (i + step) % 4) for i in range(4)])  139 us
    dot_general x23, matrix products, dot(): lax.dot_general(a, b, (((ca,), (cb,)), ((), ())), preferred_element_type=...  94.6 us
    unnamed x203, local copies, waits for them, and re-layouts  70.6 us
    ppermute x32, starting transfers between devices, swap(): return lax.ppermute(value, axis, [(0, 1), (1, 0)])  68.7 us
    ppermute x40, starting transfers between devices, px(): return lax.ppermute(value, RING, [(i, (i + step) % 4) for i in range(4)])  44.9 us
    all_gather x3, waiting for transfers between devices, gather_weights(): return lax.all_gather(pair, PLANE, axis=0, tiled=True)  33.3 us
    ppermute x32, waiting for transfers between devices, swap(): return lax.ppermute(value, axis, [(0, 1), (1, 0)])  31.8 us
  transfers between devices with their start and end apart: 78, of which 32 were waited for; matrix products, arithmetic and copies ran while one was open for 33% of the time, Pallas kernels for 0%

profile of v1, /device:TPU:1, one launch (start us, length us, event | category | flops | bytes accessed | tf_op | source)
XLA Modules:
  0.0 622.2 jit_solution(10825675530259876719)
XLA Ops:
  14.9 4.9 collective-permute-done.8
  26.6 9.0 %collective-permute-done.9 = bf16[64,1792]{0,1:T(8,128)(2,1)S(1)} collective-permute-done((bf16[64,1792]{0,1:T(8,128)(2,1)S(1)}, bf16[64,1792]{0,1:T(8,128)(2,1)S(1)}, u32[]{:S(2)}, u32[]{:S(2)}) %collective-permute-start.9) | collective-permute-done | bytes 229408 | tf_op jit(solution)/shard_map/ppermute | solution.py:21
  59.5 10.2 %collective-permute-done.16 = bf16[16,4096]{1,0:T(8,128)(2,1)S(1)} collective-permute-done((bf16[16,4096]{1,0:T(8,128)(2,1)S(1)}, bf16[16,4096]{1,0:T(8,128)(2,1)S(1)}, u32[]{:S(2)}, u32[]{:S(2)}) %collective-permute-start.16) | collective-permute-done | bytes 131104 | tf_op jit(solution)/shard_map/ppermute | solution.py:17
  80.0 10.6 %collective-permute-start.4 = (bf16[128,2048]{1,0:T(8,128)(2,1)S(1)}, bf16[128,2048]{1,0:T(8,128)(2,1)S(1)}, u32[]{:S(2)}, u32[]{:S(2)}) collective-permute-start(bf16[128,2048]{1,0:T(8,128)(2,1)S(1)} %collective-permute-done.3), channel_id=1, source_target_pairs={{0,1},{1,0},{2,3},{3,2},{4,5},{5,4},{6,7},{7,6},{8,9},{9,8},{10,11... | collective-permute-start | bytes 1572872 | tf_op jit(solution)/shard_map/ppermute | solution.py:21
  103.6 6.7 %fusion.36 = bf16[1024,768]{1,0:T(8,128)(2,1)S(1)} fusion(bf16[2048,896]{0,1:T(8,128)(2,1)} %all-gather.4.cloned.1.call-done, bf16[1024,2048]{1,0:T(8,128)(2,1)} %constant_dynamic-update-slice_fusion, f32[2048]{0:T(1024)S(1)} %bitcast.443), kind=kOutput, calls=%fused_computation.85 | convolution fusion | flops 3228303360 | bytes 8921088 | tf_op jit(solution)/shard_map/dot_general | solution.py:25
  120.7 33.3 %all-gather.6.cloned.1.call-done = bf16[2048,1792]{0,1:T(8,128)(2,1)} async-done(((bf16[128,1792]{0,1:T(8,128)(2,1)}), bf16[2048,1792]{0,1:T(8,128)(2,1)}) %all-gather.6.cloned.1.call-update) | async-done | bytes 7340048 | tf_op jit(solution)/shard_map/all_gather | solution.py:120
  172.2 6.0 collective-permute-done.19
  183.2 11.5 %collective-permute-done.38 = bf16[128,2048]{0,1:T(8,128)(2,1)S(1)} collective-permute-done((bf16[128,2048]{0,1:T(8,128)(2,1)}, bf16[128,2048]{0,1:T(8,128)(2,1)S(1)}, u32[]{:S(2)}, u32[]{:S(2)}) %collective-permute-start.38) | collective-permute-done | bytes 524320 | tf_op jit(solution)/shard_map/ppermute | solution.py:17
  202.4 7.4 %collective-permute-done.41 = bf16[64,2048]{0,1:T(8,128)(2,1)S(1)} collective-permute-done((bf16[64,2048]{0,1:T(8,128)(2,1)}, bf16[64,2048]{0,1:T(8,128)(2,1)S(1)}, u32[]{:S(2)}, u32[]{:S(2)}) %collective-permute-start.41) | collective-permute-done | bytes 262176 | tf_op jit(solution)/shard_map/ppermute | solution.py:17
  222.1 11.9 %collective-permute-done.11 = bf16[128,2048]{1,0:T(8,128)(2,1)S(1)} collective-permute-done((bf16[128,2048]{1,0:T(8,128)(2,1)S(1)}, bf16[128,2048]{1,0:T(8,128)(2,1)S(1)}, u32[]{:S(2)}, u32[]{:S(2)}) %collective-permute-start.11) | collective-permute-done | bytes 524320 | tf_op jit(solution)/shard_map/ppermute | solution.py:17
  234.0 9.7 %collective-permute-start.37 = (bf16[128,2048]{0,1:T(8,128)(2,1)}, bf16[128,2048]{0,1:T(8,128)(2,1)}, u32[]{:S(2)}, u32[]{:S(2)}) collective-permute-start(bf16[128,2048]{0,1:T(8,128)(2,1)} %collective-permute-done.36), channel_id=1, source_target_pairs={{0,1},{1,0},{2,3},{3,2},{4,5},{5,4},{6,7},{7,6},{8,9},{9,8},{10,11... | collective-permute-start | bytes 1572872 | tf_op jit(solution)/shard_map/ppermute | solution.py:21
  255.6 7.2 %concatenate.153 = bf16[1024,2048]{0,1:T(8,128)(2,1)} concatenate(bf16[128,2048]{0,1:T(8,128)(2,1)} %bitcast.57, bf16[128,2048]{0,1:T(8,128)(2,1)} %collective-permute-done.35, bf16[128,2048]{0,1:T(8,128)(2,1)} %collective-permute-done.36, bf16[128,2048]{0,1:T(8,128)(2,1)} %collective-permute-done.37, bf16[128,2048]{0,1:T(8,128)(2,1)} %copy-done.22, ...), dimensions={0} | concatenate | bytes 8388608 | tf_op jit(solution)/shard_map/concatenate | solution.py:35
  284.2 27.3 %multiply_convert_fusion.1 = (bf16[1024,1024]{1,0:T(8,128)(2,1)S(1)}, f32[1024,1024]{1,0:T(8,128)S(1)}, f32[1024,1024]{1,0:T(8,128)}) fusion(bf16[1024,2048]{1,0:T(8,128)(2,1)} %constant_dynamic-update-slice_fusion.28, bf16[2048,2048]{0,1:T(8,128)(2,1)} %all-gather.8.cloned.1.call-done), kind=kOutput, calls=%fused_computation.12 | convolution fusion | flops 4363124736 | bytes 18874368 | tf_op jit(solution)/shard_map/dot_general | solution.py:25
  311.5 6.3 %convolution_convert_fusion.2 = bf16[2048,1024]{0,1:T(8,128)(2,1)} fusion(bf16[1024,2048]{0,1:T(8,128)(2,1)S(1)} %copy-done.12, bf16[1024,1024]{1,0:T(8,128)(2,1)S(1)} %get-tuple-element.80), kind=kOutput, calls=%fused_computation.28 | convolution fusion | flops 4297064448 | bytes 10485760 | tf_op jit(solution)/shard_map/dot_general | solution.py:25
  317.8 7.6 %add_convert_fusion = bf16[1024,1024]{1,0:T(8,128)(2,1)S(1)} fusion(f32[1024,1024]{1,0:T(8,128)S(1)} %get-tuple-element.81, f32[1024,1024]{1,0:T(8,128)} %get-tuple-element.261, bf16[1024,2048]{0,1:T(8,128)(2,1)S(1)} %copy-done.12, bf16[2048,2048]{0,1:T(8,128)(2,1)S(1)} %copy-done.58), kind=kOutput, calls=%fused_computation.11 | convolution fusion | flops 4309647360 | bytes 18874368 | tf_op jit(solution)/shard_map/dot_general | solution.py:25
  325.4 5.1 convolution_convert_fusion.4
  333.7 4.7 convolution_convert_fusion.5
  342.9 6.4 %convolution_convert_fusion.3 = bf16[2048,1024]{0,1:T(8,128)(2,1)} fusion(bf16[1024,2048]{1,0:T(8,128)(2,1)S(1)} %copy-done.52, bf16[1024,1024]{1,0:T(8,128)(2,1)S(1)} %add_convert_fusion), kind=kOutput, calls=%fused_computation.29 | convolution fusion | flops 4297064448 | bytes 10485760 | tf_op jit(solution)/shard_map/dot_general | solution.py:25
  349.3 8.5 %pad_maximum_fusion = bf16[2048,2048]{0,1:T(8,128)(2,1)} fusion(bf16[2048,1024]{0,1:T(8,128)(2,1)} %convolution_convert_fusion.2, bf16[2048,1024]{0,1:T(8,128)(2,1)} %convolution_convert_fusion.3), kind=kLoop, calls=%fused_computation.3 | loop fusion | flops 16777216 | bytes 16777216 | tf_op jit(solution)/shard_map/concatenate | solution.py:219
  357.7 12.3 %copy.301 = bf16[2048,2048]{1,0:T(8,128)(2,1)} copy(bf16[2048,2048]{0,1:T(8,128)(2,1)} %pad_maximum_fusion) | data formatting | bytes 16777216
  381.7 5.5 collective-permute-done.44
  388.7 12.2 %collective-permute-done.45 = bf16[128,2048]{1,0:T(8,128)(2,1)S(1)} collective-permute-done((bf16[128,2048]{1,0:T(8,128)(2,1)S(1)}, bf16[128,2048]{1,0:T(8,128)(2,1)S(1)}, u32[]{:S(2)}, u32[]{:S(2)}) %collective-permute-start.45) | collective-permute-done | bytes 524320 | tf_op jit(solution)/shard_map/ppermute | solution.py:17
  401.6 8.1 %collective-permute-done.32 = bf16[128,2048]{1,0:T(8,128)(2,1)S(1)} collective-permute-done((bf16[128,2048]{1,0:T(8,128)(2,1)S(1)}, bf16[128,2048]{1,0:T(8,128)(2,1)S(1)}, u32[]{:S(2)}, u32[]{:S(2)}) %collective-permute-start.32) | collective-permute-done | bytes 524320 | tf_op jit(solution)/shard_map/ppermute | solution.py:17
  411.2 11.7 %collective-permute-done.33 = bf16[128,2048]{1,0:T(8,128)(2,1)S(1)} collective-permute-done((bf16[128,2048]{1,0:T(8,128)(2,1)S(1)}, bf16[128,2048]{1,0:T(8,128)(2,1)S(1)}, u32[]{:S(2)}, u32[]{:S(2)}) %collective-permute-start.33) | collective-permute-done | bytes 524320 | tf_op jit(solution)/shard_map/ppermute | solution.py:17
  430.8 9.4 %collective-permute-done.50 = bf16[128,2048]{1,0:T(8,128)(2,1)S(1)} collective-permute-done((bf16[128,2048]{1,0:T(8,128)(2,1)S(1)}, bf16[128,2048]{1,0:T(8,128)(2,1)S(1)}, u32[]{:S(2)}, u32[]{:S(2)}) %collective-permute-start.50) | collective-permute-done | bytes 524320 | tf_op jit(solution)/shard_map/ppermute | solution.py:17
  473.8 4.9 fusion.18
  487.8 13.7 %copy.299 = bf16[2048,2560]{1,0:T(8,128)(2,1)} copy(bf16[2048,2560]{0,1:T(8,128)(2,1)} %fusion.19) | data formatting | bytes 20971520
  501.6 5.5 convolution_convert_fusion.1
  528.2 17.7 %collective-permute-done.56 = bf16[128,2048]{1,0:T(8,128)(2,1)S(1)} collective-permute-done((bf16[128,2048]{1,0:T(8,128)(2,1)S(1)}, bf16[128,2048]{1,0:T(8,128)(2,1)S(1)}, u32[]{:S(2)}, u32[]{:S(2)}) %collective-permute-start.56) | collective-permute-done | bytes 524320 | tf_op jit(solution)/shard_map/ppermute | solution.py:17
  552.2 4.9 all-to-all-start
  558.5 5.0 all-to-all-done
  584.7 8.4 %collective-permute-done.71 = bf16[64,2048]{0,1:T(8,128)(2,1)} collective-permute-done((bf16[64,2048]{0,1:T(8,128)(2,1)}, bf16[64,2048]{0,1:T(8,128)(2,1)}, u32[]{:S(2)}, u32[]{:S(2)}) %collective-permute-start.71) | collective-permute-done | bytes 262176 | tf_op jit(solution)/shard_map/ppermute | solution.py:21
  (530 shorter events, 291.0 us)
Async XLA Ops:
  7.2 95.6 %all-gather.4.cloned.1.call-start = ((), (), s32[]{:S(2)}) async-start(), calls=%async_computation.3 | async-start | bytes 3899392 | tf_op jit(solution)/shard_map/all_gather | solution.py:120
  20.7 133.3 %all-gather.6.cloned.1.call-start = ((), (), s32[]{:S(2)}) async-start(), calls=%async_computation.4 | async-start | bytes 7798784 | tf_op jit(solution)/shard_map/all_gather | solution.py:120
  36.7 247.5 %all-gather.8.cloned.1.call-start = ((), (), s32[]{:S(2)}) async-start(), calls=%async_computation.5 | async-start | bytes 8912896 | tf_op jit(solution)/shard_map/all_gather | solution.py:120
  41.6 34.9 %collective-permute-start.3 = (bf16[128,2048]{1,0:T(8,128)(2,1)}, bf16[128,2048]{1,0:T(8,128)(2,1)S(1)}, u32[]{:S(2)}, u32[]{:S(2)}) collective-permute-start(bf16[128,2048]{1,0:T(8,128)(2,1)} %get-tuple-element.91), channel_id=1, source_target_pairs={{0,66},{2,0},{64,2},{66,64},{1,67},{3,1},{65,3},{67,65},{4,70},{6,... | collective-permute-start | bytes 1572872 | tf_op jit(solution)/shard_map/ppermute | solution.py:17
  44.3 35.0 %collective-permute-start.1 = (bf16[128,2048]{1,0:T(8,128)(2,1)}, bf16[128,2048]{1,0:T(8,128)(2,1)S(1)}, u32[]{:S(2)}, u32[]{:S(2)}) collective-permute-start(bf16[128,2048]{1,0:T(8,128)(2,1)} %get-tuple-element.91), channel_id=1, source_target_pairs={{0,2},{2,64},{64,66},{66,0},{1,3},{3,65},{65,67},{67,1},{4,6},{6,6... | collective-permute-start | bytes 1572872 | tf_op jit(solution)/shard_map/ppermute | solution.py:17
  44.3 46.3 %collective-permute-start = (bf16[128,2048]{1,0:T(8,128)(2,1)}, bf16[128,2048]{1,0:T(8,128)(2,1)}, u32[]{:S(2)}, u32[]{:S(2)}) collective-permute-start(bf16[128,2048]{1,0:T(8,128)(2,1)} %get-tuple-element.91), channel_id=1, source_target_pairs={{0,1},{1,0},{2,3},{3,2},{4,5},{5,4},{6,7},{7,6},{8,9},{9,8},{10,11... | collective-permute-start | bytes 1572872 | tf_op jit(solution)/shard_map/ppermute | solution.py:21
  52.6 22.5 %collective-permute-start.30 = (bf16[64,2048]{0,1:T(8,128)(2,1)S(1)}, bf16[64,2048]{0,1:T(8,128)(2,1)S(1)}, u32[]{:S(2)}, u32[]{:S(2)}) collective-permute-start(bf16[64,2048]{0,1:T(8,128)(2,1)S(1)} %pad_maximum_fusion.8), channel_id=1, source_target_pairs={{0,64},{64,0},{1,65},{65,1},{2,66},{66,2},{3,67},{67,3},{4,68},{68... | collective-permute-start | bytes 786440 | tf_op jit(solution)/shard_map/ppermute | solution.py:21
  76.5 498.7 %reduce-scatter.9.cloned.1.call-start = ((), (), s32[]{:S(2)}) async-start(), calls=%async_computation.7 | async-start | bytes 8912896
  80.0 19.7 %collective-permute-start.4 = (bf16[128,2048]{1,0:T(8,128)(2,1)S(1)}, bf16[128,2048]{1,0:T(8,128)(2,1)S(1)}, u32[]{:S(2)}, u32[]{:S(2)}) collective-permute-start(bf16[128,2048]{1,0:T(8,128)(2,1)S(1)} %collective-permute-done.3), channel_id=1, source_target_pairs={{0,1},{1,0},{2,3},{3,2},{4,5},{5,4},{6,7},{7,6},{8,9},{9,8},{10,11... | collective-permute-start | bytes 1572872 | tf_op jit(solution)/shard_map/ppermute | solution.py:21
  158.5 56.9 %collective-permute-start.10 = (bf16[4,128,2048]{2,1,0:T(8,128)(2,1)}, bf16[4,128,2048]{2,1,0:T(8,128)(2,1)}, u32[]{:S(2)}, u32[]{:S(2)}) collective-permute-start(bf16[4,128,2048]{2,1,0:T(8,128)(2,1)} %slice_bitcast_fusion.6), channel_id=1, source_target_pairs={{0,1},{1,0},{2,3},{3,2},{4,5},{5,4},{6,7},{7,6},{8,9},{9,8},{10,11... | collective-permute-start | bytes 6291464 | tf_op jit(solution)/shard_map/ppermute | solution.py:21
  179.3 34.7 %collective-permute-start.21 = (bf16[4,64,2048]{2,1,0:T(8,128)(2,1)}, bf16[4,64,2048]{2,1,0:T(8,128)(2,1)}, u32[]{:S(2)}, u32[]{:S(2)}) collective-permute-start(bf16[4,64,2048]{2,1,0:T(8,128)(2,1)} %get-tuple-element.138), channel_id=1, source_target_pairs={{0,1},{1,0},{2,3},{3,2},{4,5},{5,4},{6,7},{7,6},{8,9},{9,8},{10,11... | collective-permute-start | bytes 3145736 | tf_op jit(solution)/shard_map/ppermute | solution.py:21
  199.2 52.3 %collective-permute-start.35 = (bf16[128,2048]{0,1:T(8,128)(2,1)}, bf16[128,2048]{0,1:T(8,128)(2,1)}, u32[]{:S(2)}, u32[]{:S(2)}) collective-permute-start(bf16[128,2048]{0,1:T(8,128)(2,1)} %bitcast.57), channel_id=1, source_target_pairs={{0,1},{1,0},{2,3},{3,2},{4,5},{5,4},{6,7},{7,6},{8,9},{9,8},{10,11... | collective-permute-start | bytes 1572872 | tf_op jit(solution)/shard_map/ppermute | solution.py:21
  209.8 42.3 %collective-permute-start.39 = (bf16[128,2048]{0,1:T(8,128)(2,1)}, bf16[128,2048]{0,1:T(8,128)(2,1)}, u32[]{:S(2)}, u32[]{:S(2)}) collective-permute-start(bf16[128,2048]{0,1:T(8,128)(2,1)} %copy-done.22), channel_id=1, source_target_pairs={{0,1},{1,0},{2,3},{3,2},{4,5},{5,4},{6,7},{7,6},{8,9},{9,8},{10,11... | collective-permute-start | bytes 1572872 | tf_op jit(solution)/shard_map/ppermute | solution.py:21
  220.2 23.4 %collective-permute-start.13 = (bf16[128,2048]{1,0:T(8,128)(2,1)S(1)}, bf16[128,2048]{1,0:T(8,128)(2,1)S(1)}, u32[]{:S(2)}, u32[]{:S(2)}) collective-permute-start(bf16[128,2048]{1,0:T(8,128)(2,1)S(1)} %get-tuple-element.114), channel_id=1, source_target_pairs={{0,64},{2,66},{64,0},{66,2},{1,65},{3,67},{65,1},{67,3},{4,68},{6,... | collective-permute-start | bytes 1572872 | tf_op jit(solution)/shard_map/ppermute | solution.py:17
  220.2 25.9 %collective-permute-start.12 = (bf16[128,2048]{1,0:T(8,128)(2,1)S(1)}, bf16[128,2048]{1,0:T(8,128)(2,1)S(1)}, u32[]{:S(2)}, u32[]{:S(2)}) collective-permute-start(bf16[128,2048]{1,0:T(8,128)(2,1)S(1)} %get-tuple-element.115), channel_id=1, source_target_pairs={{0,2},{2,64},{64,66},{66,0},{1,3},{3,65},{65,67},{67,1},{4,6},{6,6... | collective-permute-start | bytes 1572872 | tf_op jit(solution)/shard_map/ppermute | solution.py:17
  234.0 21.6 %collective-permute-start.37 = (bf16[128,2048]{0,1:T(8,128)(2,1)}, bf16[128,2048]{0,1:T(8,128)(2,1)}, u32[]{:S(2)}, u32[]{:S(2)}) collective-permute-start(bf16[128,2048]{0,1:T(8,128)(2,1)} %collective-permute-done.36), channel_id=1, source_target_pairs={{0,1},{1,0},{2,3},{3,2},{4,5},{5,4},{6,7},{7,6},{8,9},{9,8},{10,11... | collective-permute-start | bytes 1572872 | tf_op jit(solution)/shard_map/ppermute | solution.py:21
  252.1 17.8 %collective-permute-start.22 = (bf16[128,2048]{1,0:T(8,128)(2,1)}, bf16[128,2048]{1,0:T(8,128)(2,1)}, u32[]{:S(2)}, u32[]{:S(2)}) collective-permute-start(bf16[128,2048]{1,0:T(8,128)(2,1)} %get-tuple-element.83), channel_id=1, source_target_pairs={{0,1},{1,0},{2,3},{3,2},{4,5},{5,4},{6,7},{7,6},{8,9},{9,8},{10,11... | collective-permute-start | bytes 1572872 | tf_op jit(solution)/shard_map/ppermute | solution.py:21
  333.3 36.8 %collective-permute-start.43 = (bf16[4,128,2048]{2,1,0:T(8,128)(2,1)}, bf16[4,128,2048]{2,1,0:T(8,128)(2,1)}, u32[]{:S(2)}, u32[]{:S(2)}) collective-permute-start(bf16[4,128,2048]{2,1,0:T(8,128)(2,1)} %slice_bitcast_fusion.2), channel_id=1, source_target_pairs={{0,1},{1,0},{2,3},{3,2},{4,5},{5,4},{6,7},{7,6},{8,9},{9,8},{10,11... | collective-permute-start | bytes 6291464 | tf_op jit(solution)/shard_map/ppermute | solution.py:21
  342.0 33.2 %collective-permute-start.31 = (bf16[4,128,2048]{2,1,0:T(8,128)(2,1)}, bf16[4,128,2048]{2,1,0:T(8,128)(2,1)}, u32[]{:S(2)}, u32[]{:S(2)}) collective-permute-start(bf16[4,128,2048]{2,1,0:T(8,128)(2,1)} %slice_bitcast_fusion.4), channel_id=1, source_target_pairs={{0,1},{1,0},{2,3},{3,2},{4,5},{5,4},{6,7},{7,6},{8,9},{9,8},{10,11... | collective-permute-start | bytes 6291464 | tf_op jit(solution)/shard_map/ppermute | solution.py:21
  370.1 224.9 %reduce-scatter.7.cloned.1.call-start = ((), (), s32[]{:S(2)}) async-start(), calls=%async_computation.6 | async-start | bytes 11141120
  374.3 26.6 %collective-permute-start.45 = (bf16[128,2048]{1,0:T(8,128)(2,1)S(1)}, bf16[128,2048]{1,0:T(8,128)(2,1)S(1)}, u32[]{:S(2)}, u32[]{:S(2)}) collective-permute-start(bf16[128,2048]{1,0:T(8,128)(2,1)S(1)} %get-tuple-element.107), channel_id=1, source_target_pairs={{0,2},{2,64},{64,66},{66,0},{1,3},{3,65},{65,67},{67,1},{4,6},{6,6... | collective-permute-start | bytes 1572872 | tf_op jit(solution)/shard_map/ppermute | solution.py:17
  378.2 31.5 %collective-permute-start.32 = (bf16[128,2048]{1,0:T(8,128)(2,1)S(1)}, bf16[128,2048]{1,0:T(8,128)(2,1)S(1)}, u32[]{:S(2)}, u32[]{:S(2)}) collective-permute-start(bf16[128,2048]{1,0:T(8,128)(2,1)S(1)} %get-tuple-element.108), channel_id=1, source_target_pairs={{0,66},{2,0},{64,2},{66,64},{1,67},{3,1},{65,3},{67,65},{4,70},{6,... | collective-permute-start | bytes 1572872 | tf_op jit(solution)/shard_map/ppermute | solution.py:17
  380.5 30.7 %collective-permute-start.34 = (bf16[128,2048]{1,0:T(8,128)(2,1)S(1)}, bf16[128,2048]{1,0:T(8,128)(2,1)S(1)}, u32[]{:S(2)}, u32[]{:S(2)}) collective-permute-start(bf16[128,2048]{1,0:T(8,128)(2,1)S(1)} %get-tuple-element.109), channel_id=1, source_target_pairs={{0,64},{2,66},{64,0},{66,2},{1,65},{3,67},{65,1},{67,3},{4,68},{6,... | collective-permute-start | bytes 1572872 | tf_op jit(solution)/shard_map/ppermute | solution.py:17
  387.2 35.7 %collective-permute-start.33 = (bf16[128,2048]{1,0:T(8,128)(2,1)S(1)}, bf16[128,2048]{1,0:T(8,128)(2,1)S(1)}, u32[]{:S(2)}, u32[]{:S(2)}) collective-permute-start(bf16[128,2048]{1,0:T(8,128)(2,1)S(1)} %get-tuple-element.110), channel_id=1, source_target_pairs={{0,2},{2,64},{64,66},{66,0},{1,3},{3,65},{65,67},{67,1},{4,6},{6,6... | collective-permute-start | bytes 1572872 | tf_op jit(solution)/shard_map/ppermute | solution.py:17
  430.7 20.6 %collective-permute-start.59 = (bf16[4,64,2048]{2,1,0:T(8,128)(2,1)S(1)}, bf16[4,64,2048]{2,1,0:T(8,128)(2,1)S(1)}, u32[]{:S(2)}, u32[]{:S(2)}) collective-permute-start(bf16[4,64,2048]{2,1,0:T(8,128)(2,1)S(1)} %pad_maximum_fusion.2), channel_id=1, source_target_pairs={{0,1},{1,0},{2,3},{3,2},{4,5},{5,4},{6,7},{7,6},{8,9},{9,8},{10,11... | collective-permute-start | bytes 3145736 | tf_op jit(solution)/shard_map/ppermute | solution.py:21
  452.6 17.5 %collective-permute-start.62 = (bf16[64,2048]{1,0:T(8,128)(2,1)}, bf16[64,2048]{1,0:T(8,128)(2,1)}, u32[]{:S(2)}, u32[]{:S(2)}) collective-permute-start(bf16[64,2048]{1,0:T(8,128)(2,1)} %get-tuple-element.130), channel_id=1, source_target_pairs={{0,64},{2,66},{64,0},{66,2},{1,65},{3,67},{65,1},{67,3},{4,68},{6,... | collective-permute-start | bytes 786440 | tf_op jit(solution)/shard_map/ppermute | solution.py:17
  452.6 17.5 %collective-permute-start.61 = (bf16[64,2048]{1,0:T(8,128)(2,1)}, bf16[64,2048]{1,0:T(8,128)(2,1)}, u32[]{:S(2)}, u32[]{:S(2)}) collective-permute-start(bf16[64,2048]{1,0:T(8,128)(2,1)} %get-tuple-element.131), channel_id=1, source_target_pairs={{0,66},{2,0},{64,2},{66,64},{1,67},{3,1},{65,3},{67,65},{4,70},{6,... | collective-permute-start | bytes 786440 | tf_op jit(solution)/shard_map/ppermute | solution.py:17
  520.4 25.4 %collective-permute-start.56 = (bf16[128,2048]{1,0:T(8,128)(2,1)S(1)}, bf16[128,2048]{1,0:T(8,128)(2,1)S(1)}, u32[]{:S(2)}, u32[]{:S(2)}) collective-permute-start(bf16[128,2048]{1,0:T(8,128)(2,1)S(1)} %get-tuple-element.102), channel_id=1, source_target_pairs={{0,66},{2,0},{64,2},{66,64},{1,67},{3,1},{65,3},{67,65},{4,70},{6,... | collective-permute-start | bytes 1572872 | tf_op jit(solution)/shard_map/ppermute | solution.py:17
  523.7 22.2 %collective-permute-start.58 = (bf16[128,2048]{1,0:T(8,128)(2,1)S(1)}, bf16[128,2048]{1,0:T(8,128)(2,1)S(1)}, u32[]{:S(2)}, u32[]{:S(2)}) collective-permute-start(bf16[128,2048]{1,0:T(8,128)(2,1)S(1)} %get-tuple-element.103), channel_id=1, source_target_pairs={{0,64},{2,66},{64,0},{66,2},{1,65},{3,67},{65,1},{67,3},{4,68},{6,... | collective-permute-start | bytes 1572872 | tf_op jit(solution)/shard_map/ppermute | solution.py:17
  523.7 26.4 %collective-permute-start.57 = (bf16[128,2048]{1,0:T(8,128)(2,1)S(1)}, bf16[128,2048]{1,0:T(8,128)(2,1)S(1)}, u32[]{:S(2)}, u32[]{:S(2)}) collective-permute-start(bf16[128,2048]{1,0:T(8,128)(2,1)S(1)} %get-tuple-element.104), channel_id=1, source_target_pairs={{0,2},{2,64},{64,66},{66,0},{1,3},{3,65},{65,67},{67,1},{4,6},{6,6... | collective-permute-start | bytes 1572872 | tf_op jit(solution)/shard_map/ppermute | solution.py:17
  524.4 32.7 %collective-permute-start.64 = (bf16[8,4096]{1,0:T(8,128)(2,1)S(1)}, bf16[8,4096]{1,0:T(8,128)(2,1)S(1)}, u32[]{:S(2)}, u32[]{:S(2)}) collective-permute-start(bf16[8,4096]{1,0:T(8,128)(2,1)S(1)} %get-tuple-element.201), channel_id=1, source_target_pairs={{0,66},{2,0},{64,2},{66,64},{1,67},{3,1},{65,3},{67,65},{4,70},{6,... | collective-permute-start | bytes 196616 | tf_op jit(solution)/shard_map/ppermute | solution.py:17
  526.5 30.7 %collective-permute-start.66 = (bf16[8,4096]{1,0:T(8,128)(2,1)S(1)}, bf16[8,4096]{1,0:T(8,128)(2,1)S(1)}, u32[]{:S(2)}, u32[]{:S(2)}) collective-permute-start(bf16[8,4096]{1,0:T(8,128)(2,1)S(1)} %get-tuple-element.202), channel_id=1, source_target_pairs={{0,64},{2,66},{64,0},{66,2},{1,65},{3,67},{65,1},{67,3},{4,68},{6,... | collective-permute-start | bytes 196616 | tf_op jit(solution)/shard_map/ppermute | solution.py:17
  (107 other events, 1305.4 us)
Sparse Core Ops, SparseCore 0:
  20.9 58.0 all-gather.3
  81.6 72.4 all-gather.5
  156.2 77.7 all-gather.7
  370.2 80.2 reduce-scatter.8
  501.7 89.1 reduce-scatter.6
